TPU v7x, 256 devices: a whole 4x4x8 slice. The times are simulated.
256 devices in a mesh: dp: 128 (over x, y_lo, z, core), tensor: 2 (over y_hi).
Axes of the slice: x: 4, y: 4 (y_hi: 2, y_lo: 2; y = y_hi * 2 + y_lo), z: 8, core: 2. Of those that a mesh axis runs over, the one named last changes fastest.
Arguments:
- hidden: bfloat16 [147456, 320], P('dp', 'tensor'), may hold values from -0.4375 to 0.4375
- cotangent: bfloat16 [147456, 4096], P('dp', 'tensor'), may hold values from -6 to 6
- down_weight: bfloat16 [320, 4096], P('tensor'), may hold values from -0.09375 to 0.09375
- momentum: float32 [128, 320, 4096], P('dp', 'tensor'), may hold values from -6 to 6
Outputs:
- update: bfloat16 [320, 4096], P('tensor')
- momentum_out: float32 [128, 320, 4096], P('dp', 'tensor')
- hidden_grad: bfloat16 [147456, 320], P('dp', 'tensor')
All inputs are finite; a program needn't handle non-finite values.
Results may differ from a plain program's by a relative error of at most 0.001.
Values may be sent and summed in bfloat16 or wider, within the bound.
No kernel may reach another device: no remote copies, remote signals or barrier semaphores. Data moves between devices by JAX's collectives and lax.ppermute only.
A program may use at most 128 MiB of HBM per device.

v0:
```python
import jax
import jax.numpy as jnp
from jax import lax
from jax.sharding import PartitionSpec as P

BLOCK = 256
BAND = 8


decay_rate = 0.9


def cosine_table():
    freq = jnp.arange(BAND, dtype=jnp.float32)[:, None]
    place = jnp.arange(BLOCK, dtype=jnp.float32)[None, :]
    scales = jnp.where(freq == 0.0, jnp.sqrt(1.0 / BLOCK), jnp.sqrt(2.0 / BLOCK))
    return scales * jnp.cos(jnp.pi * (place + 0.5) * freq / BLOCK)


def encode(accumulated, cosines):
    flattened = accumulated.reshape(-1, BLOCK)
    return lax.dot_general(
        cosines, flattened, (((1,), (1,)), ((), ())), precision=lax.Precision.HIGHEST
    )


def decode(coefficients, cosines, row_count, width):
    blocks = lax.dot_general(
        coefficients, cosines, (((0,), (0,)), ((), ())), precision=lax.Precision.HIGHEST
    )
    return blocks.reshape(row_count, width)


def body(hidden, cotangent, down_weight, momentum):
    row_count = hidden.shape[1]
    width = down_weight.shape[1]
    cosines = cosine_table()
    gathered = lax.all_gather(cotangent, "tensor", axis=1, tiled=True)
    gradient = lax.dot_general(
        hidden, gathered, (((0,), (0,)), ((), ())), preferred_element_type=jnp.float32
    )
    hidden_grad = lax.dot_general(
        gathered, down_weight, (((1,), (1,)), ((), ())), preferred_element_type=jnp.float32
    ).astype(jnp.bfloat16)
    accumulated = decay_rate * momentum[0] + gradient
    coefficients = encode(accumulated, cosines)
    remainder = accumulated - decode(coefficients, cosines, row_count, width)
    columns = coefficients.shape[1]
    summed = jnp.sum(
        lax.all_gather(coefficients, "dp", axis=0, tiled=True).reshape(-1, BAND, columns), axis=0
    )
    update = decode(summed, cosines, row_count, width).astype(jnp.bfloat16)
    return (update, remainder[None], hidden_grad)


def solution(mesh):
    placed = (P("dp", "tensor"), P("dp", "tensor"), P("tensor", None), P("dp", "tensor", None))
    return jax.shard_map(
        body,
        mesh=mesh,
        in_specs=placed,
        out_specs=(P("tensor", None), P("dp", "tensor", None), P("dp", "tensor")),
        check_vma=False,
    )
```

profile of v0, /device:TPU:1, one launch (start us, length us, event | category | flops | bytes accessed | tf_op | source)
XLA Modules:
  0.0 392.1 jit_solution(7345449321481194225)
XLA Ops:
  7.2 0.0 copy-start
  7.2 0.0 copy-start.3
  7.2 0.0 all-gather.3.cloned.1.call-start
  7.2 0.7 all-gather.3.cloned.1.call-update
  7.9 0.0 all-gather.5.cloned.1.call-start
  8.0 130.3 %all-gather.3.cloned.1.call-done = bf16[1152,4096]{1,0:T(8,128)(2,1)} async-done(((bf16[1152,2048]{1,0:T(8,128)(2,1)}), bf16[1152,4096]{1,0:T(8,128)(2,1)}) %all-gather.3.cloned.1.call-update) | async-done | bytes 9437200 | tf_op jit(solution)/shard_map/all_gather | solution.py:38
  138.3 0.0 copy-done.3
  138.3 7.9 %convolution_add_fusion = f32[160,4096]{1,0:T(8,128)} fusion(bf16[1152,160]{0,1:T(8,128)(2,1)S(1)} %copy-done.3, bf16[1152,4096]{1,0:T(8,128)(2,1)} %all-gather.3.cloned.1.call-done, f32[1,160,4096]{2,1,0:T(8,128)} %param.7), kind=kOutput, calls=%fused_computation.1 | convolution fusion | flops 1511260160 | bytes 15048704 | tf_op jit(solution)/shard_map/dot_general | solution.py:39
  146.2 3.7 reshape.33
  149.9 4.6 %fusion.1 = f32[8,2560]{1,0:T(8,128)} fusion(f32[2560,256]{1,0:T(8,128)} %reshape.33, f32[256]{0:T(256)S(1)} %add_multiply_fusion, f32[8]{0:T(128)S(1)} %compare_select_fusion), kind=kOutput, calls=%fused_computation.7 | convolution fusion | flops 62920704 | bytes 2704416 | tf_op jit(solution)/shard_map/dot_general | solution.py:22
  154.5 0.0 all-gather.5.cloned.1.call-update
  154.6 4.7 %fusion = f32[2560,256]{1,0:T(8,128)} fusion(f32[8,2560]{1,0:T(8,128)} %fusion.1, f32[256]{0:T(256)S(1)} %add_multiply_fusion, f32[8]{0:T(128)S(1)} %compare_select_fusion), kind=kOutput, calls=%fused_computation.6 | convolution fusion | flops 62920704 | bytes 2704416 | tf_op jit(solution)/shard_map/dot_general | solution.py:28
  159.2 3.8 reshape.35
  163.0 0.0 copy-done
  163.0 0.0 copy-start.1
  163.0 0.0 copy-start.2
  163.0 7.8 %convolution_convert_fusion.1 = bf16[1152,160]{0,1:T(8,128)(2,1)} fusion(bf16[1152,4096]{1,0:T(8,128)(2,1)} %all-gather.3.cloned.1.call-done, bf16[160,4096]{1,0:T(8,128)(2,1)S(1)} %copy-done), kind=kOutput, calls=%fused_computation.4 | convolution fusion | flops 1510133760 | bytes 11116544 | tf_op jit(solution)/shard_map/dot_general | solution.py:42
  170.8 0.0 copy-done.1
  170.8 0.0 copy-done.2
  170.8 1.8 subtract_bitcast_fusion
  172.6 204.5 %all-gather.5.cloned.1.call-done = f32[1024,2560]{1,0:T(8,128)} async-done(((f32[8,2560]{1,0:T(8,128)}), f32[1024,2560]{1,0:T(8,128)}) %all-gather.5.cloned.1.call-update) | async-done | bytes 10485776 | tf_op jit(solution)/shard_map/all_gather | solution.py:50
  377.1 4.5 %bitcast_reduce_fusion = f32[8,2560]{1,0:T(8,128)S(1)} fusion(f32[1024,2560]{1,0:T(8,128)} %all-gather.5.cloned.1.call-done), kind=kLoop, calls=%fused_computation | loop fusion | flops 2600960 | bytes 10567680 | tf_op jit(solution)/shard_map/reduce_sum | solution.py:49
  381.6 2.2 convolution_convert_fusion
  383.8 1.5 convert_element_type.10
  (2 shorter events, 0.0 us)
Async XLA Ops:
  7.2 155.8 %copy-start = (bf16[160,4096]{1,0:T(8,128)(2,1)S(1)}, bf16[160,4096]{1,0:T(8,128)(2,1)}, u32[]{:S(2)}) copy-start(bf16[160,4096]{1,0:T(8,128)(2,1)} %param.6) | copy-start | bytes 3932164
  7.2 131.1 %copy-start.3 = (bf16[1152,160]{0,1:T(8,128)(2,1)S(1)}, bf16[1152,160]{0,1:T(8,128)(2,1)}, u32[]{:S(2)}) copy-start(bf16[1152,160]{0,1:T(8,128)(2,1)} %param.4) | copy-start | bytes 1105924
  7.2 131.1 %all-gather.3.cloned.1.call-start = ((), (), s32[]{:S(2)}) async-start(), calls=%async_computation | async-start | bytes 14155776 | tf_op jit(solution)/shard_map/all_gather | solution.py:38
  7.9 369.2 %all-gather.5.cloned.1.call-start = ((), (), s32[]{:S(2)}) async-start(), calls=%async_computation.1 | async-start | bytes 10567680 | tf_op jit(solution)/shard_map/all_gather | solution.py:50
  163.0 7.8 %copy-start.1 = (f32[160,4096]{1,0:T(8,128)S(1)}, f32[160,4096]{1,0:T(8,128)}, u32[]{:S(2)}) copy-start(f32[160,4096]{1,0:T(8,128)} %convolution_add_fusion) | copy-start | bytes 7864324
  163.0 7.8 %copy-start.2 = (f32[160,4096]{1,0:T(8,128)S(1)}, f32[160,4096]{1,0:T(8,128)}, u32[]{:S(2)}) copy-start(f32[160,4096]{1,0:T(8,128)} %reshape.35) | copy-start | bytes 7864324
Sparse Core Ops, SparseCore 0:
  9.8 128.4 all-gather.2
  154.7 222.3 all-gather.4
where the time goes:
time: 393 us; the launch traced here: 392 us
  waiting for transfers between devices  335 us (85%)
  matrix products  27.2 us (7%)
  between operations  14.1 us (4%)
  local copies, waits for them, and re-layouts  9.02 us (2%)
  other arithmetic  6.29 us (2%)
    all_gather x1, waiting for transfers between devices, body(): lax.all_gather(coefficients, 'dp', axis=0, tiled=True)  204 us
    all_gather x1, waiting for transfers between devices, body(): gathered = lax.all_gather(cotangent, 'tensor', axis=1, tiled=True)  130 us
    dot_general x1, matrix products, body(): lax.dot_general(hidden, gathered, (((0,), (0,)), ((), ())), preferred_ele...  7.88 us
  transfers between devices with their start and end apart: 2, of which 2 were waited for; matrix products, arithmetic and copies ran while one was open for 5% of the time, Pallas kernels for 0%

commit v1 on v0

v1 whole, which is shorter than its diff:
```python
import jax
import jax.numpy as jnp
import numpy as np
from jax import lax
from jax.experimental import pallas as pl
from jax.experimental.pallas import tpu as pltpu
from jax.sharding import Mesh
from jax.sharding import PartitionSpec as P

BLOCK = 256
BAND = 8
FINE = ("x", "ylo", "z", "core", "tensor")
FINE_SIZES = (4, 2, 8, 2, 2)
DP = ("x", "ylo", "z", "core")
PLANE = ("x", "ylo")
LINE = ("z", "core", "tensor")
GRANT = 48 * 1024 * 1024

decay_rate = 0.9


def cosine_table():
    freq = np.arange(BAND, dtype=np.float64)[:, None]
    place = np.arange(BLOCK, dtype=np.float64)[None, :]
    scales = np.where(freq == 0.0, np.sqrt(1.0 / BLOCK), np.sqrt(2.0 / BLOCK))
    return scales * np.cos(np.pi * (place + 0.5) * freq / BLOCK)


def halves(table):
    high = table.astype(np.float32).astype(jnp.bfloat16)
    low = (table - high.astype(np.float64)).astype(np.float32).astype(jnp.bfloat16)
    return high, low


def split(value):
    high = value.astype(jnp.bfloat16)
    low = (value - high.astype(jnp.float32)).astype(jnp.bfloat16)
    return high, low


def dot(left, right):
    return jnp.dot(left, right, preferred_element_type=jnp.float32)


def dot_t(left, right):
    return lax.dot_general(left, right, (((1,), (1,)), ((), ())), preferred_element_type=jnp.float32)


def encode(high, low, cosines):
    both = dot_t(cosines, high) + dot_t(cosines, low)
    return both[:BAND] + both[BAND:]


def band_of(high, low, projection_ref):
    return (
        dot(high, projection_ref[0]) + dot(low, projection_ref[0]) + dot(high, projection_ref[1])
    )


def own_kernel(
    place_ref, hidden_ref, cotangent_ref, weight_ref, near_ref, far_ref, cosines_ref,
    projection_ref, remainder_ref, partial_ref, coefficients_ref,
):
    t = place_ref[0]
    tile = cotangent_ref[...]
    accumulated = decay_rate * near_ref[...] + dot(hidden_ref[...], tile)
    high, low = split(accumulated)
    remainder_ref[...] = accumulated - band_of(high, low, projection_ref)
    coefficients_ref[0, t] = encode(high, low, cosines_ref[...])
    high, low = split(decay_rate * far_ref[...])
    coefficients_ref[0, 1 - t] = encode(high, low, cosines_ref[...])
    partial = dot_t(weight_ref[...], tile)

    @pl.when(pl.program_id(0) == 0)
    def _():
        partial_ref[...] = partial

    @pl.when(pl.program_id(0) > 0)
    def _():
        partial_ref[...] += partial


def gradient_kernel(hidden_ref, cotangent_ref, coefficients_ref, cosines_ref, gradient_ref, band_ref):
    gradient = dot(hidden_ref[...], cotangent_ref[...])
    gradient_ref[...] = gradient
    band_ref[0, :2] = coefficients_ref[0]
    band_ref[0, 2] = encode(*split(gradient), cosines_ref[...])


def partial_kernel(place_ref, first_ref, second_ref, cotangent_ref, partial_ref):
    step = pl.program_id(0)
    half = pl.num_programs(0) // 2
    weight = jnp.where(step < half, first_ref[...], second_ref[...])
    partial = dot_t(weight, cotangent_ref[...])

    @pl.when(step == 0)
    def _():
        partial_ref[...] = partial

    @pl.when(step > 0)
    def _():
        partial_ref[...] += partial


def far_kernel(place_ref, held_ref, far_ref, gradient_ref, projection_ref, remainder_ref):
    accumulated = decay_rate * far_ref[...] + gradient_ref[...]
    high, low = split(accumulated)
    remainder_ref[...] = accumulated - band_of(high, low, projection_ref)


def update_kernel(summed_ref, cosines_ref, update_ref):
    for block in range(summed_ref.shape[0] * 2):
        update_ref[:, block * BLOCK : (block + 1) * BLOCK] = lax.dot_general(
            summed_ref[block % 8, block // 8], cosines_ref[...], (((0,), (0,)), ((), ())),
            precision=lax.Precision.HIGHEST, preferred_element_type=jnp.float32,
        ).astype(jnp.bfloat16)


def body(hidden, cotangent, down_weight, momentum):
    f32 = jnp.float32
    rows, width = down_weight.shape
    tokens, features = cotangent.shape
    tiles = features // BLOCK
    t = lax.axis_index("tensor")
    core = lax.axis_index("core")
    place = jnp.stack([t, core]).astype(jnp.int32)
    momentum = momentum.reshape(rows, width)
    table = cosine_table()
    cosines = jnp.asarray(np.concatenate(halves(table)))
    projection = jnp.asarray(np.stack(halves(table.T @ table)))
    swap = [(0, 1), (1, 0)]
    params = pltpu.CompilerParams(dimension_semantics=("arbitrary",), vmem_limit_bytes=GRANT)

    def grid(scalars, in_specs, out_specs):
        return pltpu.PrefetchScalarGridSpec(
            num_scalar_prefetch=scalars, grid=(tiles,), in_specs=in_specs, out_specs=out_specs
        )

    def whole(shape):
        return pl.BlockSpec(shape, lambda j, *_: (0,) * len(shape))

    near = pl.BlockSpec((rows, BLOCK), lambda j, place: (0, place[0] * tiles + j))
    far = pl.BlockSpec((rows, BLOCK), lambda j, place: (0, (1 - place[0]) * tiles + j))
    tile = pl.BlockSpec((tokens, BLOCK), lambda j, *_: (0, j))
    row_tile = pl.BlockSpec((rows, BLOCK), lambda j, *_: (0, j))

    own_hidden = hidden.T
    their_hidden = lax.ppermute(own_hidden, "tensor", swap)
    half = features // 2
    sent = lax.dynamic_slice(down_weight, (0, (1 - t) * features + core * half), (rows, half))
    first = lax.ppermute(sent, ("ylo", "tensor"), [(0, 3), (3, 0), (1, 2), (2, 1)])
    second = lax.ppermute(first, "core", swap)

    remainder, own_partial, coefficients = pl.pallas_call(
        own_kernel,
        grid_spec=grid(
            1,
            [whole((rows, tokens)), tile, near, near, far, whole((2 * BAND, BLOCK)), whole((2, BLOCK, BLOCK))],
            [near, whole((rows, tokens)), pl.BlockSpec((1, 2, BAND, rows), lambda j, *_: (j, 0, 0, 0))],
        ),
        out_shape=[
            jax.ShapeDtypeStruct((rows, width), f32),
            jax.ShapeDtypeStruct((rows, tokens), f32),
            jax.ShapeDtypeStruct((tiles, 2, BAND, rows), f32),
        ],
        compiler_params=params,
        cost_estimate=pl.CostEstimate(flops=4 * rows * tokens * features, bytes_accessed=12 << 20, transcendentals=0),
        name="own_half",
    )(place, own_hidden, cotangent, down_weight, momentum, momentum, cosines, projection)

    gradient, band = pl.pallas_call(
        gradient_kernel,
        grid_spec=grid(
            0,
            [whole((rows, tokens)), tile, pl.BlockSpec((1, 2, BAND, rows), lambda j: (j, 0, 0, 0)), whole((2 * BAND, BLOCK))],
            [row_tile, pl.BlockSpec((1, 3, BAND, rows), lambda j: (j, 0, 0, 0))],
        ),
        out_shape=[
            jax.ShapeDtypeStruct((rows, features), f32),
            jax.ShapeDtypeStruct((tiles, 3, BAND, rows), f32),
        ],
        compiler_params=params,
        cost_estimate=pl.CostEstimate(flops=2 * rows * tokens * features, bytes_accessed=7 << 20, transcendentals=0),
        name="their_gradient",
    )(their_hidden, cotangent, coefficients, cosines)
    far_gradient = lax.ppermute(gradient, "tensor", swap)

    partial = pl.pallas_call(
        partial_kernel,
        grid_spec=grid(
            1,
            [
                pl.BlockSpec((rows, BLOCK), lambda j, place: (0, jnp.minimum(j, tiles // 2 - 1))),
                pl.BlockSpec((rows, BLOCK), lambda j, place: (0, jnp.maximum(j - tiles // 2, 0))),
                pl.BlockSpec((tokens, BLOCK), lambda j, place: (0, (place[1] * (tiles // 2) + j) % tiles)),
            ],
            whole((rows, tokens)),
        ),
        out_shape=jax.ShapeDtypeStruct((rows, tokens), f32),
        compiler_params=params,
        cost_estimate=pl.CostEstimate(flops=2 * rows * tokens * features, bytes_accessed=6 << 20, transcendentals=0),
        name="their_partial",
    )(place, first, second, cotangent)
    far_partial = lax.ppermute(partial, "tensor", swap)

    spread = lax.all_to_all(band, PLANE, 0, 0, tiled=True)
    total = jnp.sum(spread, axis=0)
    slot = jnp.arange(2)[:, None, None]
    across = jnp.where(slot == t, total[2][None], 0.0)
    partner = (jnp.arange(32) % 2)[:, None, None, None] == t
    payload = jnp.where(partner, total[None, :2], across[None])
    total = jnp.sum(lax.all_to_all(payload, LINE, 0, 0, tiled=True), axis=0)
    payload = jnp.broadcast_to(total[None], (8,) + total.shape)
    summed = lax.all_to_all(payload, PLANE, 0, 0, tiled=True)

    update = pl.pallas_call(
        update_kernel,
        out_shape=jax.ShapeDtypeStruct((rows, width), jnp.bfloat16),
        compiler_params=pltpu.CompilerParams(vmem_limit_bytes=GRANT),
        name="update",
    )(summed, jnp.asarray(table.astype(np.float32)))

    remainder = pl.pallas_call(
        far_kernel,
        grid_spec=grid(
            1,
            [pl.BlockSpec(memory_space=pl.ANY), far, row_tile, whole((2, BLOCK, BLOCK))],
            far,
        ),
        out_shape=jax.ShapeDtypeStruct((rows, width), f32),
        input_output_aliases={1: 0},
        compiler_params=params,
        cost_estimate=pl.CostEstimate(flops=0, bytes_accessed=4 << 20, transcendentals=0),
        name="far_half",
    )(place, remainder, momentum, far_gradient, projection)

    hidden_grad = (own_partial + far_partial).astype(jnp.bfloat16).T
    return (update, remainder[None], hidden_grad)


def solution(mesh):
    fine = Mesh(mesh.devices.reshape(FINE_SIZES), FINE)
    return jax.shard_map(
        body,
        mesh=fine,
        in_specs=(P(DP, "tensor"), P(DP, "tensor"), P("tensor", None), P(DP, "tensor", None)),
        out_specs=(P("tensor", None), P(DP, "tensor", None), P(DP, "tensor")),
        check_vma=False,
    )
```

time: 393 us -> 114 us (0.29)
  waiting for transfers between devices: 335 us -> 1.1 us
  blocking collectives: 0 us -> 50.1 us
  Pallas kernels: 0 us -> 31 us
  matrix products: 27.2 us -> 0 us
  starting transfers between devices: 0.08 us -> 16 us
  between operations: 14.1 us -> 0.71 us
    all_gather x2 -> x0, waiting for transfers between devices: 335 us -> none  [the longest x1 204 us: body(): lax.all_gather(coefficients, 'dp', axis=0, tiled=True)]
    all_to_all x0 -> x2, blocking collectives: none -> 50.1 us  [the longest x1 40.8 us: body(): total = jnp.sum(lax.all_to_all(payload, LINE, 0, 0, tiled=True), axis=0)]
    pallas_call x0 -> x5, Pallas kernels: none -> 31 us  [the longest x1 10.6 us: body(): pl.pallas_call(own_kernel, grid_spec=grid(1, [whole((rows, tokens)), tile...]
    dot_general x5 -> x0, matrix products: 27.2 us -> none  [the longest x1 7.88 us: body(): lax.dot_general(hidden, gathered, (((0,), (0,)), ((), ())), preferred_ele...]
    ppermute x0 -> x5, starting transfers between devices: none -> 12 us  [the longest x1 3.83 us: body(): their_hidden = lax.ppermute(own_hidden, 'tensor', swap)]
    unnamed x8 -> x20, local copies, waits for them, and re-layouts: 0.02 us -> 9.12 us
    reshape x2 -> x0, local copies, waits for them, and re-layouts: 7.53 us -> none  [the longest x1 3.79 us: decode(): return blocks.reshape(row_count, width)]
    all_to_all x0 -> x1, starting transfers between devices: none -> 4.02 us  [body(): spread = lax.all_to_all(band, PLANE, 0, 0, tiled=True)]
  transfers between devices with their start and end apart: 2 -> 6, of which waited for: 2 -> 1; matrix products, arithmetic and copies ran while one was open for 5% -> 4% of each run, Pallas kernels for 0% -> 23%
where the time goes in v1:
time: 114 us; the launch traced here: 112 us
  blocking collectives  50.1 us (44%)
  Pallas kernels  31 us (27%)
  starting transfers between devices  16 us (14%)
  local copies, waits for them, and re-layouts  10.1 us (9%)
  other arithmetic  3.31 us (3%)
    all_to_all x1, blocking collectives, body(): total = jnp.sum(lax.all_to_all(payload, LINE, 0, 0, tiled=True), axis=0)  40.8 us
    pallas_call x1, Pallas kernels, body(): pl.pallas_call(own_kernel, grid_spec=grid(1, [whole((rows, tokens)), tile...  10.6 us
    all_to_all x1, blocking collectives, body(): summed = lax.all_to_all(payload, PLANE, 0, 0, tiled=True)  9.35 us
    unnamed x20, local copies, waits for them, and re-layouts  9.12 us
    pallas_call x1, Pallas kernels, body(): pl.pallas_call(gradient_kernel, grid_spec=grid(0, [whole((rows, tokens)),...  7.5 us
    pallas_call x1, Pallas kernels, body(): pl.pallas_call(partial_kernel, grid_spec=grid(1, [pl.BlockSpec((rows, BLO...  4.99 us
    pallas_call x1, Pallas kernels, body(): pl.pallas_call(far_kernel, grid_spec=grid(1, [pl.BlockSpec(memory_space=p...  4.57 us
    all_to_all x1, starting transfers between devices, body(): spread = lax.all_to_all(band, PLANE, 0, 0, tiled=True)  4.02 us
  transfers between devices with their start and end apart: 6, of which 1 were waited for; matrix products, arithmetic and copies ran while one was open for 4% of the time, Pallas kernels for 23%

profile of v1, /device:TPU:1, one launch (start us, length us, event | category | flops | bytes accessed | tf_op | source)
XLA Modules:
  0.0 112.4 jit_solution(1008996149173712562)
XLA Ops:
  0.6 3.8 %collective-permute-start = (bf16[160,1152]{1,0:T(8,128)(2,1)}, bf16[160,1152]{1,0:T(8,128)(2,1)S(1)}, u32[]{:S(2)}, u32[]{:S(2)}) collective-permute-start(bf16[160,1152]{1,0:T(8,128)(2,1)} %bitcast.12), channel_id=1, source_target_pairs={{0,1},{1,0},{2,3},{3,2},{4,5},{5,4},{6,7},{7,6},{8,9},{9,8},{10,11... | collective-permute-start | bytes 1105928 | tf_op jit(solution)/shard_map/ppermute | solution.py:148
  4.5 1.0 constant_dynamic-slice_fusion
  5.5 0.9 collective-permute-start.2
  6.4 1.7 %copy-done.1 = f32[1,160,4096]{2,1,0:T(8,128)S(1)} copy-done((f32[1,160,4096]{2,1,0:T(8,128)S(1)}, f32[1,160,4096]{2,1,0:T(8,128)}, u32[]{:S(2)}) %copy-start.1) | copy-done | bytes 2621464
  8.1 1.3 %copy-done.3 = bf16[160,4096]{1,0:T(8,128)(2,1)S(1)} copy-done((bf16[160,4096]{1,0:T(8,128)(2,1)S(1)}, bf16[160,4096]{1,0:T(8,128)(2,1)}, u32[]{:S(2)}) %copy-start.3) | copy-done | bytes 1310744
  9.5 0.9 copy-done.4
  10.4 1.0 copy-done.6
  11.4 0.7 copy-done.7
  12.1 10.6 %own_half.1 = (f32[160,4096]{1,0:T(8,128)}, f32[160,1152]{1,0:T(8,128)S(1)}, f32[8,2,8,160]{3,2,1,0:T(8,128)S(1)}) custom-call(s32[2]{0:T(128)S(1)} %pad_add_fusion.place_ref, bf16[160,1152]{1,0:T(8,128)(2,1)S(1)} %bitcast.13, bf16[1152,2048]{1,0:T(8,128)(2,1)} %cotangent_ref.5, bf16[160,4096]{1,0:T(8,128)(2,1)S(1)} %copy-done.3, f32[160,4096]{1,0:T(8,128)S(1)} %bitcast.9, ...), custom_call_target="tpu_custom_call" | custom-call | flops 1509949440 | bytes 12582912 | tf_op jit(solution)/shard_map/own_half/pallas_call | solution.py:154
  22.7 7.5 %their_gradient.1 = (f32[160,2048]{1,0:T(8,128)S(1)}, f32[8,3,8,160]{3,2,1,0:T(8,128)}) custom-call(bf16[160,1152]{1,0:T(8,128)(2,1)S(1)} %collective-permute-done.hidden_ref, bf16[1152,2048]{1,0:T(8,128)(2,1)} %cotangent_ref.5, f32[8,2,8,160]{3,2,1,0:T(8,128)S(1)} %get-tuple-element.8.coefficients_ref, bf16[16,256]{1,0:T(8,128)(2,1)S(1)} %copy-done.7), custom_call_target="tpu_custom_call" | custom-call | flops 754974720 | bytes 7340032 | tf_op jit(solution)/shard_map/their_gradient/pallas_call | solution.py:171
  30.2 1.1 copy-done.9
  31.2 4.0 %all-to-all-start = ((f32[8,3,8,160]{3,2,1,0:T(8,128)}), f32[8,3,8,160]{3,2,1,0:T(8,128)S(1)}, u32[]{:S(2)}, u32[]{:S(2)}) async-start(f32[8,3,8,160]{3,2,1,0:T(8,128)} %get-tuple-element.9), calls=%async_computation | async-start | bytes 393216 | tf_op jit(solution)/shard_map/all_to_all | solution.py:206
  35.3 1.6 %collective-permute-start.3 = (bf16[160,1024]{1,0:T(8,128)(2,1)S(1)}, bf16[160,1024]{1,0:T(8,128)(2,1)S(1)}, u32[]{:S(2)}, u32[]{:S(2)}) collective-permute-start(bf16[160,1024]{1,0:T(8,128)(2,1)S(1)} %collective-permute-done.2.first_ref), channel_id=1, source_target_pairs={{0,2},{2,0},{1,3},{3,1},{4,6},{6,4},{5,7},{7,5},{8,10},{10,8},{9,1... | collective-permute-start | bytes 983048 | tf_op jit(solution)/shard_map/ppermute | solution.py:152
  36.9 2.8 %collective-permute-start.1 = (f32[160,2048]{1,0:T(8,128)}, f32[160,2048]{1,0:T(8,128)S(1)}, u32[]{:S(2)}, u32[]{:S(2)}) collective-permute-start(f32[160,2048]{1,0:T(8,128)} %copy-done.9), channel_id=1, source_target_pairs={{0,1},{1,0},{2,3},{3,2},{4,5},{5,4},{6,7},{7,6},{8,9},{9,8},{10,11... | collective-permute-start | bytes 3932168 | tf_op jit(solution)/shard_map/ppermute | solution.py:186
  39.7 1.1 all-to-all-done
  40.9 2.3 %copy-done = bf16[1152,2048]{1,0:T(8,128)(2,1)S(1)} copy-done((bf16[1152,2048]{1,0:T(8,128)(2,1)S(1)}, bf16[1152,2048]{1,0:T(8,128)(2,1)}, u32[]{:S(2)}) %copy-start) | copy-done | bytes 4718616
  43.3 5.0 %their_partial.1 = f32[160,1152]{1,0:T(8,128)S(1)} custom-call(s32[2]{0:T(128)S(1)} %pad_add_fusion.place_ref, bf16[160,1024]{1,0:T(8,128)(2,1)S(1)} %collective-permute-done.2.first_ref, bf16[160,1024]{1,0:T(8,128)(2,1)S(1)} %collective-permute-done.3.second_ref, bf16[1152,2048]{1,0:T(8,128)(2,1)S(1)} %copy-done), custom_call_target="tpu_custom_call" | custom-call | flops 754974720 | bytes 6291456 | tf_op jit(solution)/shard_map/their_partial/pallas_call | solution.py:188
  48.3 2.9 %collective-permute-start.4 = (f32[160,1152]{1,0:T(8,128)S(1)}, f32[160,1152]{1,0:T(8,128)}, u32[]{:S(2)}, u32[]{:S(2)}) collective-permute-start(f32[160,1152]{1,0:T(8,128)S(1)} %their_partial.1), channel_id=1, source_target_pairs={{0,1},{1,0},{2,3},{3,2},{4,5},{5,4},{6,7},{7,6},{8,9},{9,8},{10,11... | collective-permute-start | bytes 2211848 | tf_op jit(solution)/shard_map/ppermute | solution.py:204
  51.3 40.8 %all_to_all.15 = f32[32,2,8,160]{3,2,1,0:T(8,128)} all-to-all(f32[32,2,8,160]{3,2,1,0:T(8,128)S(1)} %broadcast_select_fusion), channel_id=1, replica_groups=mesh['x'=4,'ylo'=2,'z'=8,'core'=2,'tensor'=2] {'z','core','tensor'}, dimensions={0} | all-to-all | bytes 655360 | tf_op jit(solution)/shard_map/all_to_all | solution.py:212
  92.0 1.1 reduce_sum.19
  93.1 9.4 %all_to_all.16.summed_ref = f32[8,2,8,160]{3,2,1,0:T(8,128)S(1)} all-to-all(f32[8,2,8,160]{3,2,1,0:T(8,128)S(1)} %broadcast_in_dim.66), channel_id=1, replica_groups=mesh['x'=4,'ylo'=2,'z'=8,'core'=2,'tensor'=2] {'x','ylo'}, dimensions={0} | all-to-all | bytes 163840 | tf_op jit(solution)/shard_map/all_to_all | solution.py:214
  102.5 3.3 %update.1 = bf16[160,4096]{1,0:T(8,128)(2,1)} custom-call(f32[8,2,8,160]{3,2,1,0:T(8,128)S(1)} %all_to_all.16.summed_ref, f32[8,256]{1,0:T(8,128)S(1)} %copy-done.8), custom_call_target="tpu_custom_call" | custom-call | tf_op jit(solution)/shard_map/update/pallas_call | solution.py:216
  105.8 1.9 %fusion = bf16[1152,160]{0,1:T(8,128)(2,1)} fusion(f32[160,1152]{1,0:T(8,128)S(1)} %get-tuple-element.12, f32[160,1152]{1,0:T(8,128)} %collective-permute-done.4), kind=kLoop, calls=%fused_computation.1 | loop fusion | flops 368640 | bytes 1843200 | tf_op jit(solution)/shard_map/transpose | solution.py:237
  107.8 4.6 %far_half.1 = f32[160,4096]{1,0:T(8,128)} custom-call(s32[2]{0:T(128)S(1)} %pad_add_fusion.place_ref, f32[160,4096]{1,0:T(8,128)} %get-tuple-element.10.held_ref, f32[160,4096]{1,0:T(8,128)S(1)} %bitcast.11, f32[160,2048]{1,0:T(8,128)S(1)} %collective-permute-done.1.gradient_ref, bf16[2,256,256]{2,1,0:T(8,128)(2,1)S(1)} %copy-done.5), custom_call_target="tpu_custom_call", output_to_operand_aliasing={{}: (1, {})} | custom-call | bytes 4194304 | tf_op jit(solution)/shard_map/far_half/pallas_call | solution.py:223
  (27 shorter events, 0.3 us)
Async XLA Ops:
  0.6 22.0 %collective-permute-start = (bf16[160,1152]{1,0:T(8,128)(2,1)}, bf16[160,1152]{1,0:T(8,128)(2,1)S(1)}, u32[]{:S(2)}, u32[]{:S(2)}) collective-permute-start(bf16[160,1152]{1,0:T(8,128)(2,1)} %bitcast.12), channel_id=1, source_target_pairs={{0,1},{1,0},{2,3},{3,2},{4,5},{5,4},{6,7},{7,6},{8,9},{9,8},{10,11... | collective-permute-start | bytes 1105928 | tf_op jit(solution)/shard_map/ppermute | solution.py:148
  5.5 29.8 %collective-permute-start.2 = (bf16[160,1024]{1,0:T(8,128)(2,1)S(1)}, bf16[160,1024]{1,0:T(8,128)(2,1)S(1)}, u32[]{:S(2)}, u32[]{:S(2)}) collective-permute-start(bf16[160,1024]{1,0:T(8,128)(2,1)S(1)} %constant_dynamic-slice_fusion), channel_id=1, source_target_pairs={{0,33},{33,0},{1,32},{32,1},{2,35},{35,2},{3,34},{34,3},{4,37},{37... | collective-permute-start | bytes 983048 | tf_op jit(solution)/shard_map/ppermute | solution.py:151
  6.4 1.7 %copy-start.1 = (f32[1,160,4096]{2,1,0:T(8,128)S(1)}, f32[1,160,4096]{2,1,0:T(8,128)}, u32[]{:S(2)}) copy-start(f32[1,160,4096]{2,1,0:T(8,128)} %param.10) | copy-start | bytes 7864324
  8.1 1.3 %copy-start.3 = (bf16[160,4096]{1,0:T(8,128)(2,1)S(1)}, bf16[160,4096]{1,0:T(8,128)(2,1)}, u32[]{:S(2)}) copy-start(bf16[160,4096]{1,0:T(8,128)(2,1)} %weight_ref.1) | copy-start | bytes 3932164
  9.5 0.9 copy-start.4
  10.4 1.0 copy-start.6
  11.4 0.7 copy-start.7
  30.2 1.1 copy-start.9
  31.2 9.5 %all-to-all-start = ((f32[8,3,8,160]{3,2,1,0:T(8,128)}), f32[8,3,8,160]{3,2,1,0:T(8,128)S(1)}, u32[]{:S(2)}, u32[]{:S(2)}) async-start(f32[8,3,8,160]{3,2,1,0:T(8,128)} %get-tuple-element.9), calls=%async_computation | async-start | bytes 393216 | tf_op jit(solution)/shard_map/all_to_all | solution.py:206
  35.3 5.6 %collective-permute-start.3 = (bf16[160,1024]{1,0:T(8,128)(2,1)S(1)}, bf16[160,1024]{1,0:T(8,128)(2,1)S(1)}, u32[]{:S(2)}, u32[]{:S(2)}) collective-permute-start(bf16[160,1024]{1,0:T(8,128)(2,1)S(1)} %collective-permute-done.2.first_ref), channel_id=1, source_target_pairs={{0,2},{2,0},{1,3},{3,1},{4,6},{6,4},{5,7},{7,5},{8,10},{10,8},{9,1... | collective-permute-start | bytes 983048 | tf_op jit(solution)/shard_map/ppermute | solution.py:152
  36.9 70.9 %collective-permute-start.1 = (f32[160,2048]{1,0:T(8,128)}, f32[160,2048]{1,0:T(8,128)S(1)}, u32[]{:S(2)}, u32[]{:S(2)}) collective-permute-start(f32[160,2048]{1,0:T(8,128)} %copy-done.9), channel_id=1, source_target_pairs={{0,1},{1,0},{2,3},{3,2},{4,5},{5,4},{6,7},{7,6},{8,9},{9,8},{10,11... | collective-permute-start | bytes 3932168 | tf_op jit(solution)/shard_map/ppermute | solution.py:186
  40.9 2.3 %copy-start = (bf16[1152,2048]{1,0:T(8,128)(2,1)S(1)}, bf16[1152,2048]{1,0:T(8,128)(2,1)}, u32[]{:S(2)}) copy-start(bf16[1152,2048]{1,0:T(8,128)(2,1)} %cotangent_ref.5) | copy-start | bytes 14155780
  48.3 54.2 %copy-start.8 = (f32[8,256]{1,0:T(8,128)S(1)}, f32[8,256]{1,0:T(8,128)}, u32[]{:S(2)}) copy-start(f32[8,256]{1,0:T(8,128)} %constant.40.clone.cosines_ref) | copy-start | bytes 24580
  48.3 57.6 %collective-permute-start.4 = (f32[160,1152]{1,0:T(8,128)S(1)}, f32[160,1152]{1,0:T(8,128)}, u32[]{:S(2)}, u32[]{:S(2)}) collective-permute-start(f32[160,1152]{1,0:T(8,128)S(1)} %their_partial.1), channel_id=1, source_target_pairs={{0,1},{1,0},{2,3},{3,2},{4,5},{5,4},{6,7},{7,6},{8,9},{9,8},{10,11... | collective-permute-start | bytes 2211848 | tf_op jit(solution)/shard_map/ppermute | solution.py:204
  102.5 5.3 %copy-start.2 = (f32[1,160,4096]{2,1,0:T(8,128)S(1)}, f32[1,160,4096]{2,1,0:T(8,128)}, u32[]{:S(2)}) copy-start(f32[1,160,4096]{2,1,0:T(8,128)} %param.10) | copy-start | bytes 7864324
  102.5 5.3 %copy-start.5 = (bf16[2,256,256]{2,1,0:T(8,128)(2,1)S(1)}, bf16[2,256,256]{2,1,0:T(8,128)(2,1)}, u32[]{:S(2)}) copy-start(bf16[2,256,256]{2,1,0:T(8,128)(2,1)} %constant.39.clone.projection_ref) | copy-start | bytes 786436
